TPU v7x, 512 devices: a whole 4x4x16 slice. The times are simulated.
512 devices in a mesh: col: 128 (over y, z, core), row: 4 (over x).
Axes of the slice: x: 4, y: 4, z: 16, core: 2. Of those that a mesh axis runs over, the one named last changes fastest.
Arguments:
- right_side: float32 [5, 256, 4096], P(None, 'col'), may hold values from -6 to 6
- diag_inverse: float32 [5, 256, 4096], P(None, 'col'), may hold values from -1 to 2
- panels: bfloat16 [4, 256, 64, 2048], P(None, 'col', None, 'row'), may hold values from -0.125 to 0.125
- tile_rows: int32 [4, 256, 32], P(None, 'col', 'row'), may hold values from 256 to 1279, as said below
Outputs:
- solution: float32 [5, 256, 4096], P(None, 'col')
Inputs may be any that keep to these rules, and one draw needn't show every extreme that they name: tile_rows[t, q, s] is the global index of a block column of a level above t. Tiles of the same t whose block columns q share q // 2, whose s share s // 8, and whose block rows i share (i % 256) // 2, all name the same block row.
All inputs are finite; a program needn't handle non-finite values.
Results may differ from a plain program's by a relative error of at most 0.0059.
Values may be sent and summed in bfloat16 or wider, within the bound.
A program may use at most 64 MiB of HBM per device.

v0:
```python
import jax
import jax.numpy as jnp
from jax import lax
from jax.sharding import PartitionSpec as P

BS = 64
R = 64
LEVELS = 5
BPL = 2
NNZ_DEV = 8
TLEV = 4


def solve_blocks(partial_value, right_blocks, inverse, transpose):
    highest = lax.Precision.HIGHEST
    form = "jba,jbr->jar" if transpose else "jab,jbr->jar"
    if partial_value is None:
        return jnp.einsum(form, inverse, right_blocks, precision=highest)
    summed = lax.psum(partial_value, "row")
    return jnp.einsum(form, inverse, right_blocks - summed, precision=highest)


def local(right_side, diag_inverse, panels, tile_rows):
    owners = lax.axis_size("col")
    cols_level = BPL * owners
    slots_all = LEVELS * BPL
    tiles_dev = BPL * NNZ_DEV
    right_blocks = right_side.reshape(LEVELS, BPL, BS, R)
    inverse = diag_inverse.reshape(LEVELS, BPL, BS, BS)
    targets = tile_rows.reshape(TLEV, tiles_dev)
    local_position = targets % cols_level
    owner_of = local_position // BPL
    row_codes = targets // cols_level * BPL + local_position % BPL
    updates = jnp.zeros((slots_all + 1, BS * R), jnp.float32)
    solved_levels = []
    landings = []
    for height in range(LEVELS):
        if height == 0:
            partial_value = None
        else:
            partial_value = updates[height * BPL : (height + 1) * BPL].reshape(BPL, BS, R)
        forward = solve_blocks(partial_value, right_blocks[height], inverse[height], False)
        solved_levels.append(forward)
        if height < TLEV:
            rounded = forward.astype(jnp.bfloat16)
            products = lax.dot_general(
                panels[height],
                rounded,
                (((1,), (1,)), ((0,), (0,))),
                preferred_element_type=jnp.float32,
            )
            products = products.reshape(tiles_dev, BS * R)
            outgoing = jax.ops.segment_sum(products, owner_of[height], num_segments=owners)
            marks = jnp.full((owners,), -1, jnp.int32).at[owner_of[height]].max(row_codes[height])
            incoming, incoming_codes = (
                lax.all_to_all(outgoing, "col", split_axis=0, concat_axis=0, tiled=True),
                lax.all_to_all(marks, "col", split_axis=0, concat_axis=0, tiled=True),
            )
            landing = jnp.where(incoming_codes < 0, slots_all, incoming_codes)
            updates = updates + jax.ops.segment_sum(incoming, landing, num_segments=slots_all + 1)
            landings.append(landing)
    solution = jnp.zeros((slots_all + 1, BS * R), jnp.float32)
    whole_levels = jnp.zeros((LEVELS * cols_level, BS * R), jnp.bfloat16)
    for height in range(LEVELS - 1, -1, -1):
        if height < TLEV:
            picked = jnp.take(whole_levels, targets[height], axis=0)
            picked = picked.reshape(BPL, NNZ_DEV * BS, R)
            partial_value = lax.dot_general(
                panels[height],
                picked,
                (((2,), (1,)), ((0,), (0,))),
                preferred_element_type=jnp.float32,
            )
            backward = solve_blocks(partial_value, solved_levels[height], inverse[height], True)
        else:
            backward = solve_blocks(None, solved_levels[height], inverse[height], True)
        flat_blocks = backward.reshape(BPL, BS * R)
        solution = solution.at[height * BPL : (height + 1) * BPL].set(flat_blocks)
        if height > 0:
            shared = lax.all_gather(flat_blocks.astype(jnp.bfloat16), "col", axis=0, tiled=True)
            whole_levels = whole_levels.at[height * cols_level : (height + 1) * cols_level].set(
                shared
            )
    return solution[:slots_all].reshape(LEVELS, BPL, BS * R)


def solution(mesh):
    in_specs = (
        P(None, "col", None),
        P(None, "col", None),
        P(None, "col", None, "row"),
        P(None, "col", "row"),
    )
    out_specs = P(None, "col", None)
    return jax.shard_map(local, mesh=mesh, in_specs=in_specs, out_specs=out_specs, check_vma=False)
```

profile of v0, /device:TPU:1, one launch (start us, length us, event | category | flops | bytes accessed | tf_op | source)
XLA Modules:
  0.0 1295.6 jit_solution(16338217328216740449)
XLA Ops:
  9.9 20.6 %all-to-all-start = ((s32[128,1,1]{2,1,0:T(1,128)}), s32[128,1,1]{2,1,0:T(1,128)S(1)}, u32[]{:S(2)}, u32[]{:S(2)}) async-start(s32[128,1,1]{2,1,0:T(1,128)} %copy.52), calls=%async_computation | async-start | bytes 131072 | tf_op jit(solution)/shard_map/all_to_all | solution.py:57
  36.7 3.7 all_to_all.67
  40.4 5.0 all-to-all-done
  45.4 11.2 all-to-all-start.1
  58.2 2.3 reduce.18
  60.6 95.1 %all-to-all-done.1 = f32[128,1,4096]{2,1,0:T(1,128)S(1)} async-done(((f32[128,1,4096]{2,1,0:T(1,128)}), f32[128,1,4096]{2,1,0:T(1,128)S(1)}, u32[]{:S(2)}, u32[]{:S(2)}) %all-to-all-start.1) | async-done | bytes 2097184 | tf_op jit(solution)/shard_map/all_to_all | solution.py:56
  155.7 9.1 all-to-all-start.2
  164.8 4.5 scatter_custom_fusion.2
  169.4 14.6 %psum.56 = f32[2,64,64]{2,1,0:T(8,128)S(1)} all-reduce(f32[2,64,64]{2,1,0:T(8,128)S(1)} %reshape.508), channel_id=1, replica_groups=mesh['col'=128,'row'=4] {'row'}, use_global_device_ids=true, to_apply=%region_4.5 | all-reduce | flops 8192 | bytes 65536 | tf_op jit(solution)/shard_map/psum | solution.py:19
  185.6 1.8 scatter_custom_fusion.4
  187.5 3.5 copy.58
  191.0 19.1 %all-to-all-start.3 = ((f32[128,1,4096]{2,1,0:T(1,128)}), f32[128,1,4096]{2,1,0:T(1,128)S(1)}, u32[]{:S(2)}, u32[]{:S(2)}) async-start(f32[128,1,4096]{2,1,0:T(1,128)} %copy.58), calls=%async_computation.3 | async-start | bytes 4194304 | tf_op jit(solution)/shard_map/all_to_all | solution.py:56
  211.8 2.3 reduce.19
  214.2 95.0 %all-to-all-done.3 = f32[128,1,4096]{2,1,0:T(1,128)S(1)} async-done(((f32[128,1,4096]{2,1,0:T(1,128)}), f32[128,1,4096]{2,1,0:T(1,128)S(1)}, u32[]{:S(2)}, u32[]{:S(2)}) %all-to-all-start.3) | async-done | bytes 2097184 | tf_op jit(solution)/shard_map/all_to_all | solution.py:56
  309.2 9.1 all-to-all-start.4
  318.3 4.6 scatter_custom_fusion.5
  323.0 12.3 psum.57
  336.9 1.8 scatter_custom_fusion.7
  338.7 3.5 copy.62
  342.2 18.7 %all-to-all-start.5 = ((f32[128,1,4096]{2,1,0:T(1,128)}), f32[128,1,4096]{2,1,0:T(1,128)S(1)}, u32[]{:S(2)}, u32[]{:S(2)}) async-start(f32[128,1,4096]{2,1,0:T(1,128)} %copy.62), calls=%async_computation.5 | async-start | bytes 4194304 | tf_op jit(solution)/shard_map/all_to_all | solution.py:56
  363.5 2.3 reduce.20
  365.9 94.2 %all-to-all-done.5 = f32[128,1,4096]{2,1,0:T(1,128)S(1)} async-done(((f32[128,1,4096]{2,1,0:T(1,128)}), f32[128,1,4096]{2,1,0:T(1,128)S(1)}, u32[]{:S(2)}, u32[]{:S(2)}) %all-to-all-start.5) | async-done | bytes 2097184 | tf_op jit(solution)/shard_map/all_to_all | solution.py:56
  460.1 8.7 all-to-all-start.6
  468.8 4.6 scatter_custom_fusion.8
  473.5 13.8 %psum.58 = f32[2,64,64]{2,1,0:T(8,128)S(1)} all-reduce(f32[2,64,64]{2,1,0:T(8,128)S(1)} %reshape.512), channel_id=1, replica_groups=mesh['col'=128,'row'=4] {'row'}, use_global_device_ids=true, to_apply=%region_12.13 | all-reduce | flops 8192 | bytes 65536 | tf_op jit(solution)/shard_map/psum | solution.py:19
  491.6 3.5 copy.66
  495.1 19.1 %all-to-all-start.7 = ((f32[128,1,4096]{2,1,0:T(1,128)}), f32[128,1,4096]{2,1,0:T(1,128)S(1)}, u32[]{:S(2)}, u32[]{:S(2)}) async-start(f32[128,1,4096]{2,1,0:T(1,128)} %copy.66), calls=%async_computation.7 | async-start | bytes 4194304 | tf_op jit(solution)/shard_map/all_to_all | solution.py:56
  518.2 2.3 reduce.21
  520.5 92.8 %all-to-all-done.7 = f32[128,1,4096]{2,1,0:T(1,128)S(1)} async-done(((f32[128,1,4096]{2,1,0:T(1,128)}), f32[128,1,4096]{2,1,0:T(1,128)S(1)}, u32[]{:S(2)}, u32[]{:S(2)}) %all-to-all-start.7) | async-done | bytes 2097184 | tf_op jit(solution)/shard_map/all_to_all | solution.py:56
  613.3 4.6 scatter_custom_fusion.11
  618.1 11.5 psum.59
  631.2 135.9 %all-gather.9.cloned.1.call-done = bf16[128,2,4096]{2,1,0:T(2,128)(2,1)} async-done(((bf16[1,2,4096]{2,1,0:T(2,128)(2,1)}), bf16[128,2,4096]{2,1,0:T(2,128)(2,1)}) %all-gather.9.cloned.1.call-update) | async-done | bytes 2097168 | tf_op jit(solution)/shard_map/all_gather | solution.py:80
  767.1 2.7 reshape.662
  769.8 5.3 scatter.31
  775.1 6.1 gather_fusion
  781.7 13.7 %psum.60 = f32[2,64,64]{1,2,0:T(8,128)S(1)} all-reduce(f32[2,64,64]{1,2,0:T(8,128)S(1)} %convolution_bitcast_fusion.15), channel_id=1, replica_groups=mesh['col'=128,'row'=4] {'row'}, use_global_device_ids=true, to_apply=%region_16.18 | all-reduce | flops 8192 | bytes 65536 | tf_op jit(solution)/shard_map/psum | solution.py:19
  796.8 138.1 %all-gather.11.cloned.1.call-done = bf16[128,2,4096]{2,1,0:T(2,128)(2,1)} async-done(((bf16[1,2,4096]{2,1,0:T(2,128)(2,1)}), bf16[128,2,4096]{2,1,0:T(2,128)(2,1)}) %all-gather.11.cloned.1.call-update) | async-done | bytes 2097168 | tf_op jit(solution)/shard_map/all_gather | solution.py:80
  934.9 2.7 reshape.664
  939.1 6.1 gather_fusion.1
  945.8 13.7 %psum.61 = f32[2,64,64]{1,2,0:T(8,128)S(1)} all-reduce(f32[2,64,64]{1,2,0:T(8,128)S(1)} %convolution_bitcast_fusion.14), channel_id=1, replica_groups=mesh['col'=128,'row'=4] {'row'}, use_global_device_ids=true, to_apply=%region_17.19 | all-reduce | flops 8192 | bytes 65536 | tf_op jit(solution)/shard_map/psum | solution.py:19
  960.7 138.2 %all-gather.13.cloned.1.call-done = bf16[128,2,4096]{2,1,0:T(2,128)(2,1)} async-done(((bf16[1,2,4096]{2,1,0:T(2,128)(2,1)}), bf16[128,2,4096]{2,1,0:T(2,128)(2,1)}) %all-gather.13.cloned.1.call-update) | async-done | bytes 2097168 | tf_op jit(solution)/shard_map/all_gather | solution.py:80
  1098.9 2.7 reshape.666
  1103.1 6.1 gather_fusion.2
  1109.8 13.7 %psum.62 = f32[2,64,64]{1,2,0:T(8,128)S(1)} all-reduce(f32[2,64,64]{1,2,0:T(8,128)S(1)} %convolution_bitcast_fusion.13), channel_id=1, replica_groups=mesh['col'=128,'row'=4] {'row'}, use_global_device_ids=true, to_apply=%region_18.20 | all-reduce | flops 8192 | bytes 65536 | tf_op jit(solution)/shard_map/psum | solution.py:19
  1124.5 138.4 %all-gather.15.cloned.1.call-done = bf16[128,2,4096]{2,1,0:T(2,128)(2,1)} async-done(((bf16[1,2,4096]{2,1,0:T(2,128)(2,1)}), bf16[128,2,4096]{2,1,0:T(2,128)(2,1)}) %all-gather.15.cloned.1.call-update) | async-done | bytes 2097168 | tf_op jit(solution)/shard_map/all_gather | solution.py:80
  1262.9 2.7 reshape.668
  1267.1 6.1 gather_fusion.3
  1273.7 13.7 %psum.63 = f32[2,64,64]{2,1,0:T(8,128)S(1)} all-reduce(f32[2,64,64]{2,1,0:T(8,128)S(1)} %convolution_bitcast_fusion.12), channel_id=1, replica_groups=mesh['col'=128,'row'=4] {'row'}, use_global_device_ids=true, to_apply=%region_19.21 | all-reduce | flops 8192 | bytes 65536 | tf_op jit(solution)/shard_map/psum | solution.py:19
  (126 shorter events, 40.0 us)
Async XLA Ops:
  9.9 35.5 %all-to-all-start = ((s32[128,1,1]{2,1,0:T(1,128)}), s32[128,1,1]{2,1,0:T(1,128)S(1)}, u32[]{:S(2)}, u32[]{:S(2)}) async-start(s32[128,1,1]{2,1,0:T(1,128)} %copy.52), calls=%async_computation | async-start | bytes 131072 | tf_op jit(solution)/shard_map/all_to_all | solution.py:57
  45.4 110.3 %all-to-all-start.1 = ((f32[128,1,4096]{2,1,0:T(1,128)}), f32[128,1,4096]{2,1,0:T(1,128)S(1)}, u32[]{:S(2)}, u32[]{:S(2)}) async-start(f32[128,1,4096]{2,1,0:T(1,128)} %all_to_all.67), calls=%async_computation.1 | async-start | bytes 4194304 | tf_op jit(solution)/shard_map/all_to_all | solution.py:56
  56.6 127.8 %copy-start = (bf16[4,2,64,512]{3,2,1,0:T(8,128)(2,1)S(1)}, bf16[4,2,64,512]{3,2,1,0:T(8,128)(2,1)}, u32[]{:S(2)}) copy-start(bf16[4,2,64,512]{3,2,1,0:T(8,128)(2,1)} %param.26) | copy-start | bytes 1572868
  155.7 35.3 %all-to-all-start.2 = ((s32[128,1,1]{2,1,0:T(1,128)}), s32[128,1,1]{2,1,0:T(1,128)S(1)}, u32[]{:S(2)}, u32[]{:S(2)}) async-start(s32[128,1,1]{2,1,0:T(1,128)} %copy.55), calls=%async_computation.2 | async-start | bytes 131072 | tf_op jit(solution)/shard_map/all_to_all | solution.py:57
  191.0 118.2 %all-to-all-start.3 = ((f32[128,1,4096]{2,1,0:T(1,128)}), f32[128,1,4096]{2,1,0:T(1,128)S(1)}, u32[]{:S(2)}, u32[]{:S(2)}) async-start(f32[128,1,4096]{2,1,0:T(1,128)} %copy.58), calls=%async_computation.3 | async-start | bytes 4194304 | tf_op jit(solution)/shard_map/all_to_all | solution.py:56
  309.2 33.0 %all-to-all-start.4 = ((s32[128,1,1]{2,1,0:T(1,128)}), s32[128,1,1]{2,1,0:T(1,128)S(1)}, u32[]{:S(2)}, u32[]{:S(2)}) async-start(s32[128,1,1]{2,1,0:T(1,128)} %copy.59), calls=%async_computation.4 | async-start | bytes 131072 | tf_op jit(solution)/shard_map/all_to_all | solution.py:57
  342.2 117.9 %all-to-all-start.5 = ((f32[128,1,4096]{2,1,0:T(1,128)}), f32[128,1,4096]{2,1,0:T(1,128)S(1)}, u32[]{:S(2)}, u32[]{:S(2)}) async-start(f32[128,1,4096]{2,1,0:T(1,128)} %copy.62), calls=%async_computation.5 | async-start | bytes 4194304 | tf_op jit(solution)/shard_map/all_to_all | solution.py:56
  460.1 35.0 %all-to-all-start.6 = ((s32[128,1,1]{2,1,0:T(1,128)}), s32[128,1,1]{2,1,0:T(1,128)S(1)}, u32[]{:S(2)}, u32[]{:S(2)}) async-start(s32[128,1,1]{2,1,0:T(1,128)} %copy.63), calls=%async_computation.6 | async-start | bytes 131072 | tf_op jit(solution)/shard_map/all_to_all | solution.py:57
  495.1 118.2 %all-to-all-start.7 = ((f32[128,1,4096]{2,1,0:T(1,128)}), f32[128,1,4096]{2,1,0:T(1,128)S(1)}, u32[]{:S(2)}, u32[]{:S(2)}) async-start(f32[128,1,4096]{2,1,0:T(1,128)} %copy.66), calls=%async_computation.7 | async-start | bytes 4194304 | tf_op jit(solution)/shard_map/all_to_all | solution.py:56
  514.2 116.8 %copy-start.2 = (s32[4,2,8]{2,1,0:T(2,128)S(1)}, s32[4,2,8]{2,1,0:T(2,128)}, u32[]{:S(2)}) copy-start(s32[4,2,8]{2,1,0:T(2,128)} %param.27) | copy-start | bytes 772
  514.2 252.9 %all-gather.9.cloned.1.call-start = ((), (), s32[]{:S(2)}) async-start(), calls=%async_computation.8 | async-start | bytes 2113536 | tf_op jit(solution)/shard_map/all_gather | solution.py:80
  520.5 109.1 %copy-start.1 = (f32[2,64,64]{1,2,0:T(8,128)S(1)}, f32[2,64,64]{1,2,0:T(8,128)}, u32[]{:S(2)}) copy-start(f32[2,64,64]{1,2,0:T(8,128)} %copy.68) | copy-start | bytes 98308
  630.9 304.0 %all-gather.11.cloned.1.call-start = ((), (), s32[]{:S(2)}) async-start(), calls=%async_computation.9 | async-start | bytes 2113536 | tf_op jit(solution)/shard_map/all_gather | solution.py:80
  796.5 302.4 %all-gather.13.cloned.1.call-start = ((), (), s32[]{:S(2)}) async-start(), calls=%async_computation.10 | async-start | bytes 2113536 | tf_op jit(solution)/shard_map/all_gather | solution.py:80
  960.5 302.4 %all-gather.15.cloned.1.call-start = ((), (), s32[]{:S(2)}) async-start(), calls=%async_computation.11 | async-start | bytes 2113536 | tf_op jit(solution)/shard_map/all_gather | solution.py:80
Sparse Core Ops, SparseCore 0:
  631.0 135.9 all-gather.8
  796.6 138.2 all-gather.10
  960.6 138.2 all-gather.12
  1124.6 138.2 all-gather.14
where the time goes:
time: 1310 us; the launch traced here: 1300 us
  waiting for transfers between devices  933 us (71%)
  starting transfers between devices  116 us (9%)
  blocking collectives  107 us (8%)
  local copies, waits for them, and re-layouts  78.8 us (6%)
  other arithmetic  41.1 us (3%)
  between operations  14.3 us (1%)
    all_gather x4, waiting for transfers between devices, local(): lax.all_gather(flat_blocks.astype(jnp.bfloat16), 'col', axis=0, tiled=True)  550 us
    all_to_all x4, waiting for transfers between devices, local(): lax.all_to_all(outgoing, 'col', split_axis=0, concat_axis=0, tiled=True)  377 us
    psum x8, blocking collectives, solve_blocks(): summed = lax.psum(partial_value, 'row')  107 us
    all_to_all x4, starting transfers between devices, local(): lax.all_to_all(outgoing, 'col', split_axis=0, concat_axis=0, tiled=True)  68 us
    all_to_all x4, starting transfers between devices, local(): lax.all_to_all(marks, 'col', split_axis=0, concat_axis=0, tiled=True)  47.5 us
  transfers between devices with their start and end apart: 12, of which 9 were waited for; matrix products, arithmetic and copies ran while one was open for 5% of the time, Pallas kernels for 0%

commit v1 on v0

v1 whole, which is shorter than its diff:
```python
import functools

import jax
import jax.numpy as jnp
from jax import lax
from jax.experimental import pallas as pl
from jax.experimental.pallas import tpu as pltpu
from jax.sharding import PartitionSpec as P

BS = 64
LEVELS = 5
BPL = 2
NNZ_DEV = 8
TLEV = 4
RW = 8
MESH = pl.DeviceIdType.MESH
F32 = jnp.float32
BF16 = jnp.bfloat16
HIGHEST = lax.Precision.HIGHEST
NT_DIMS = (((1,), (1,)), ((), ()))
NN_DIMS = (((1,), (0,)), ((), ()))


def sizes(owners, rows):
    nz = 16 if owners % 32 == 0 else owners // 4
    ny = owners // 2 // nz
    return ny, nz


def kernel(
    owners,
    rows,
    bt,
    dd,
    tr,
    pan,
    out,
    trg,
    bu,
    ddc,
    pg,
    tbl,
    keepv,
    tbs,
    keeps,
    pd,
    cs,
    acc,
    sb,
    own,
    ry,
    sz,
    rz,
    ys,
    xu,
    xs,
    xg,
    fx,
    osc,
    cell_sem,
    pan_sem,
    loc_sem,
    tab_sem,
    y_send,
    y_recv,
    z_send,
    z_recv,
    f_send,
    f_recv,
):
    ny, nz = sizes(owners, rows)
    units = owners // 2
    cols = owners * BPL
    cells = 2 * rows
    tiles = cells * BPL * NNZ_DEV
    chunks = (TLEV * cols + 127) // 128
    col = lax.axis_index("col")
    x = lax.axis_index("row")
    c = col % 2
    z = (col // 2) % nz
    y = col // 2 // nz
    me = x * 2 + c
    unit = y * nz + z

    def at(x_to, y_to, z_to, c_to):
        return {"row": x_to, "col": (y_to * nz + z_to) * 2 + c_to}

    def cell_peer(j):
        other = (me + j) % cells
        return other, at(other // 2, y, z, other % 2)

    def y_peer(j):
        y_to = (y + j) % ny
        return y_to, at(x, y_to, z, c)

    def z_peer(j):
        half = (j + 1) // 2
        step = nz // 2 + jnp.where(j % 2 == 0, half, -half)
        z_to = (z + step) % nz
        return z_to, at(x, y, z_to, c)

    def send(src, dst, send_sem, recv_sem, device):
        pltpu.make_async_remote_copy(
            src_ref=src,
            dst_ref=dst,
            send_sem=send_sem,
            recv_sem=recv_sem,
            device_id=device,
            device_id_type=MESH,
        ).start()

    def settle(ref, sem):
        pltpu.make_async_copy(ref, ref, sem).wait()

    low = lax.broadcasted_iota(jnp.int32, (RW, 128), 1) < BS

    barrier = pltpu.get_barrier_semaphore()

    def greet(device):
        pl.semaphore_signal(barrier, inc=1, device_id=device, device_id_type=MESH)

    for j in range(1, cells):
        greet(cell_peer(j)[1])
    for j in range(1, ny):
        greet(y_peer(j)[1])

    @pl.loop(0, nz - 1)
    def _(j):
        greet(z_peer(j)[1])

    pl.semaphore_wait(barrier, cells - 1 + ny - 1 + nz - 1)

    for j in range(1, cells):
        device = cell_peer(j)[1]
        send(tr, trg.at[me], cell_sem.at[0], cell_sem.at[1], device)
    core_peer = at(x, y, z, 1 - c)
    send(bt.at[x * 2 + 1 - c], bu.at[c], cell_sem.at[2], cell_sem.at[3], core_peer)
    send(dd, ddc.at[c], cell_sem.at[4], cell_sem.at[5], core_peer)
    for t in range(TLEV):
        pltpu.make_async_copy(pan.at[t], pg.at[t, me], loc_sem.at[t]).start()
        for j in range(1, cells):
            device = cell_peer(j)[1]
            send(pan.at[t], pg.at[t, me], pan_sem.at[0, t], pan_sem.at[1, t], device)
    trg[me] = tr[...]
    bu[c] = bt[me]
    ddc[c] = dd[...]

    settle(trg.at[pl.ds(0, cells - 1)], cell_sem.at[1])
    targets = trg[0]
    for j in range(1, cells):
        targets = targets + trg[j]
    square = (128, 128)
    above = lax.broadcasted_iota(jnp.int32, square, 0)
    lane = lax.broadcasted_iota(jnp.int32, square, 1)
    for t in range(TLEV):
        mine = jnp.broadcast_to(targets[t : t + 1, :], square)
        other = mine.T
        before = (other < mine) | ((other == mine) & (above < lane))
        rank = jnp.sum(before.astype(jnp.int32), axis=0, keepdims=True)
        placed = jnp.broadcast_to(rank, square).T == lane
        order = jnp.sum(jnp.where(placed, above, 0), axis=0, keepdims=True)
        ordered = jnp.sum(jnp.where(placed, other, 0), axis=0, keepdims=True)
        ordered8 = jnp.broadcast_to(ordered, (8, 128))
        first = lax.broadcasted_iota(jnp.int32, (8, 128), 1) == 0
        same = (ordered8 == pltpu.roll(ordered8, 1, 1)) & jnp.logical_not(first)
        keepv[t : t + 1, :] = same.astype(F32)[0:1]
        tbl[t : t + 1, :] = order
        tbl[TLEV + t : TLEV + t + 1, :] = jnp.clip(mine[0:1] - cols, 0, TLEV * cols - 1)
        for chunk in range(t * cols // 128, chunks):
            slot = lane + (cols + chunk * 128)
            upto = jnp.sum((other <= slot).astype(jnp.int32), axis=0, keepdims=True)
            equal = jnp.sum((other == slot).astype(jnp.int32), axis=0, keepdims=True)
            row = 2 * TLEV + t * chunks + chunk
            tbl[row : row + 1, :] = jnp.where(equal > 0, upto - 1, 128)
    pltpu.make_async_copy(tbl, tbs, tab_sem.at[0]).start()
    pltpu.make_async_copy(keepv, keeps, tab_sem.at[1]).start()
    pltpu.make_async_copy(tbl, tbs, tab_sem.at[0]).wait()
    pltpu.make_async_copy(keepv, keeps, tab_sem.at[1]).wait()
    cs[128] = jnp.zeros((RW, 128), F32)
    settle(bu.at[0], cell_sem.at[3])
    settle(ddc.at[0], cell_sem.at[5])

    def last_sum(t, level, s):
        number = (level - 1) * cols + s
        place = tbs[2 * TLEV + t * chunks + number // 128, number % 128]
        return cs[place]

    def pair(t, level, u, h):
        s = u * 4 + 2 * h
        return jnp.where(low, last_sum(t, level, s), last_sum(t, level, s + 1))

    update = None
    for t in range(LEVELS):
        solved = []
        for core in range(2):
            remain = bu[core, t]
            if t > 0:
                remain = remain - update[core]
            value = lax.dot_general(
                remain, ddc[core, t], NT_DIMS, precision=HIGHEST, preferred_element_type=F32
            )
            ys[t, core] = value
            solved.append(value)
        if t == TLEV:
            break
        nothing = jnp.zeros((RW, 128), F32)
        left = jnp.concatenate(
            [
                jnp.where(low, solved[0], 0.0),
                jnp.where(low, 0.0, solved[0]),
                nothing,
                nothing,
            ],
            axis=0,
        )
        right = jnp.concatenate(
            [
                nothing,
                nothing,
                jnp.where(low, solved[1], 0.0),
                jnp.where(low, 0.0, solved[1]),
            ],
            axis=0,
        )
        vectors = jnp.concatenate([left, right], axis=1).astype(BF16)
        settle(pg.at[t, 0], loc_sem.at[t])
        settle(pg.at[t, pl.ds(0, cells - 1)], pan_sem.at[1, t])
        for group in range(rows):
            panel = jnp.concatenate([pg[t, 2 * group], pg[t, 2 * group + 1]], axis=0)
            product = lax.dot_general(vectors, panel, NN_DIMS, preferred_element_type=F32)
            for b in range(4):
                for p in range(4):
                    value = product[b * RW : (b + 1) * RW, p * 128 : (p + 1) * 128]
                    turned = pltpu.roll(value, BS, 1)
                    tile = group * 32 + b * 8 + p * 2
                    pd[tile] = jnp.where(low, value, turned)
                    pd[tile + 1] = jnp.where(low, turned, value)

        def scan(i, total, t=t):
            for k in range(8):
                place = i * 8 + k
                total = total * keeps[t, place] + pd[tbs[t, place]]
                cs[place] = total
            return total

        lax.fori_loop(0, tiles // 8, scan, jnp.zeros((RW, 128), F32))

        level = t + 1
        for j in list(range(1, ny)) + [0]:
            y_to, device = y_peer(j)

            @pl.loop(0, nz)
            def _(i, t=t, level=level, j=j, y_to=y_to):
                u = y_to * nz + i
                halves = []
                for h in range(2):
                    value = pair(t, level, u, h)
                    if t > 0:
                        value = value + acc[level - 2, u * 2 + h]
                    halves.append(value)
                if j == 0:
                    own[i, 0] = halves[0]
                    own[i, 1] = halves[1]
                else:
                    sb[t, u] = jnp.concatenate(halves, axis=0).astype(BF16)

            if j > 0:
                send(
                    sb.at[t, pl.ds(y_to * nz, nz)],
                    ry.at[t, j - 1],
                    y_send.at[t],
                    y_recv.at[t],
                    device,
                )
        for level in range(t + 2, LEVELS):

            @pl.loop(0, units)
            def _(u, t=t, level=level):
                for h in range(2):
                    value = pair(t, level, u, h)
                    if t > 0:
                        value = value + acc[level - 2, u * 2 + h]
                    acc[level - 2, u * 2 + h] = value

        settle(ry.at[t], y_recv.at[t])

        def partial(i, t=t):
            halves = []
            for h in range(2):
                value = own[i, h]
                for j in range(ny - 1):
                    value = value + ry[t, j, i].astype(F32)[h * RW : (h + 1) * RW]
                halves.append(value)
            return halves

        @pl.loop(0, nz - 1)
        def _(j, t=t):
            z_to, device = z_peer(j)
            sz[t, j] = jnp.concatenate(partial(z_to), axis=0).astype(BF16)
            send(sz.at[t, j], rz.at[t, j], z_send.at[t], z_recv.at[t], device)

        update = partial(z)
        settle(rz.at[t], z_recv.at[t])
        for j in range(nz - 1):
            arrived = rz[t, j].astype(F32)
            update = [update[0] + arrived[:RW], update[1] + arrived[RW:]]

    for t in range(LEVELS - 1, -1, -1):
        if t < TLEV:
            weighted = jnp.zeros((4 * RW, 4 * BS), F32)
            for group in range(rows):
                for b in range(4):
                    for p in range(4):
                        tile = group * 32 + b * 8 + p * 2
                        value = jnp.where(
                            low, xs[tbs[TLEV + t, tile]], xs[tbs[TLEV + t, tile + 1]]
                        )
                        xg[group, b * RW : (b + 1) * RW, p * 128 : (p + 1) * 128] = value
                panel = jnp.concatenate([pg[t, 2 * group], pg[t, 2 * group + 1]], axis=0)
                weighted = weighted + lax.dot_general(
                    xg[group].astype(BF16), panel, NT_DIMS, preferred_element_type=F32
                )
        results = []
        for core in range(2):
            remain = ys[t, core]
            if t < TLEV:
                remain = remain - jnp.where(
                    low,
                    weighted[core * 16 : core * 16 + 8, core * 128 : core * 128 + 128],
                    weighted[core * 16 + 8 : core * 16 + 16, core * 128 : core * 128 + 128],
                )
            value = lax.dot_general(
                remain, ddc[core, t], NN_DIMS, precision=HIGHEST, preferred_element_type=F32
            )
            fx[t, core] = value
            results.append(value)
        if t > 0:
            xu[t - 1, unit] = jnp.concatenate(results, axis=0).astype(BF16)

            @pl.loop(0, nz - 1)
            def _(j, t=t):
                z_to, device = z_peer(j)
                here = xu.at[t - 1, unit]
                send(here, here, z_send.at[TLEV + t - 1], z_recv.at[TLEV + t - 1], device)

        osc[me, t] = fx[t, c]
        for j in range(1, cells):
            other, device = cell_peer(j)
            send(fx.at[t, other % 2], osc.at[me, t], f_send, f_recv, device)

        if t > 0:

            def expand(u, t=t):
                value = xu[t - 1, u].astype(F32)
                for h in range(2):
                    half = value[h * RW : (h + 1) * RW]
                    turned = pltpu.roll(half, BS, 1)
                    slot = (t - 1) * cols + u * 4 + h * 2
                    xs[slot] = jnp.where(low, half, turned)
                    xs[slot + 1] = jnp.where(low, turned, half)

            settle(xu.at[t - 1, pl.ds(0, nz - 1)], z_recv.at[TLEV + t - 1])
            for j in range(1, ny):
                y_to, device = y_peer(j)
                here = xu.at[t - 1, pl.ds(y * nz, nz)]
                send(here, here, y_send.at[TLEV + t - 1], y_recv.at[TLEV + t - 1], device)

            @pl.loop(0, nz)
            def _(i):
                expand(y * nz + i)

            settle(xu.at[t - 1, pl.ds(0, (ny - 1) * nz)], y_recv.at[TLEV + t - 1])

            @pl.loop(0, (ny - 1) * nz)
            def _(i):
                expand((y * nz + nz + i) % units)

    settle(trg.at[pl.ds(0, cells - 1)], cell_sem.at[0])
    settle(bu.at[0], cell_sem.at[2])
    settle(ddc.at[0], cell_sem.at[4])
    for t in range(TLEV):
        settle(pg.at[t, pl.ds(0, cells - 1)], pan_sem.at[0, t])
        settle(ry.at[t], y_send.at[t])
        settle(rz.at[t], z_send.at[t])
        settle(xu.at[t, pl.ds(0, (ny - 1) * nz)], y_send.at[TLEV + t])
        settle(xu.at[t, pl.ds(0, nz - 1)], z_send.at[TLEV + t])
    settle(osc.at[pl.ds(0, cells - 1)], f_send)
    settle(osc.at[pl.ds(0, cells - 1)], f_recv)
    out[...] = osc[...]


def local(right_side, diag_inverse, panels, tile_rows):
    owners = lax.axis_size("col")
    rows = lax.axis_size("row")
    ny, nz = sizes(owners, rows)
    units = owners // 2
    cols = owners * BPL
    cells = 2 * rows
    chunks = (TLEV * cols + 127) // 128
    table_rows = 2 * TLEV + TLEV * chunks
    me = lax.axis_index("row") * 2 + lax.axis_index("col") % 2
    bt = right_side.reshape(LEVELS, BPL, BS, cells, RW).transpose(3, 0, 4, 1, 2)
    bt = bt.reshape(cells, LEVELS, RW, BPL * BS)
    inverse = diag_inverse.reshape(LEVELS, BPL, BS, BS)
    eye = jnp.eye(BPL, dtype=F32)[None, :, None, :, None]
    dd = jnp.where(eye > 0, inverse[:, :, :, None, :], 0.0).reshape(LEVELS, BPL * BS, BPL * BS)
    pan = panels.reshape(TLEV, BPL * BS, NNZ_DEV * BS)
    per = BPL * NNZ_DEV
    spread = jnp.tile(tile_rows.reshape(TLEV, per), (2, 128 // per))
    lane = lax.broadcasted_iota(jnp.int32, (8, 128), 1)
    tr = jnp.where(lane // per == me, spread, 0)
    if cells * per < 128:
        tr = jnp.where(lane >= cells * per, 1 << 20, tr)
    vmem = pl.BlockSpec(memory_space=pltpu.VMEM)
    result = pl.pallas_call(
        functools.partial(kernel, owners, rows),
        out_shape=jax.ShapeDtypeStruct((cells, LEVELS, RW, BPL * BS), F32),
        in_specs=[vmem, vmem, vmem, pl.BlockSpec(memory_space=pl.ANY)],
        out_specs=vmem,
        scratch_shapes=[
            pltpu.VMEM((cells, 8, 128), jnp.int32),
            pltpu.VMEM((2, LEVELS, RW, 128), F32),
            pltpu.VMEM((2, LEVELS, 128, 128), F32),
            pltpu.VMEM((TLEV, cells, BPL * BS, NNZ_DEV * BS), BF16),
            pltpu.VMEM((table_rows, 128), jnp.int32),
            pltpu.VMEM((8, 128), F32),
            pltpu.SMEM((table_rows, 128), jnp.int32),
            pltpu.SMEM((8, 128), F32),
            pltpu.VMEM((128, RW, 128), F32),
            pltpu.VMEM((129, RW, 128), F32),
            pltpu.VMEM((TLEV - 1, units * 2, RW, 128), F32),
            pltpu.VMEM((TLEV, units, 2 * RW, 128), BF16),
            pltpu.VMEM((nz, 2, RW, 128), F32),
            pltpu.VMEM((TLEV, ny - 1, nz, 2 * RW, 128), BF16),
            pltpu.VMEM((TLEV, nz - 1, 2 * RW, 128), BF16),
            pltpu.VMEM((TLEV, nz - 1, 2 * RW, 128), BF16),
            pltpu.VMEM((LEVELS, 2, RW, 128), F32),
            pltpu.VMEM((TLEV, units, 2 * RW, 128), BF16),
            pltpu.VMEM((TLEV * cols, RW, 128), F32),
            pltpu.VMEM((rows, 4 * RW, NNZ_DEV * BS), F32),
            pltpu.VMEM((LEVELS, 2, RW, 128), F32),
            pltpu.VMEM((cells, LEVELS, RW, 128), F32),
            pltpu.SemaphoreType.DMA((6,)),
            pltpu.SemaphoreType.DMA((2, TLEV)),
            pltpu.SemaphoreType.DMA((TLEV,)),
            pltpu.SemaphoreType.DMA((2,)),
            pltpu.SemaphoreType.DMA((2 * TLEV,)),
            pltpu.SemaphoreType.DMA((2 * TLEV,)),
            pltpu.SemaphoreType.DMA((2 * TLEV,)),
            pltpu.SemaphoreType.DMA((2 * TLEV,)),
            pltpu.SemaphoreType.DMA,
            pltpu.SemaphoreType.DMA,
        ],
        compiler_params=pltpu.CompilerParams(
            collective_id=0, has_side_effects=True, vmem_limit_bytes=40 * 1024 * 1024
        ),
    )(bt, dd, tr, pan)
    result = result.reshape(cells, LEVELS, RW, BPL, BS).transpose(1, 3, 4, 0, 2)
    return result.reshape(LEVELS, BPL, BS * cells * RW)


def solution(mesh):
    in_specs = (
        P(None, "col", None),
        P(None, "col", None),
        P(None, "col", None, "row"),
        P(None, "col", "row"),
    )
    out_specs = P(None, "col", None)
    return jax.shard_map(local, mesh=mesh, in_specs=in_specs, out_specs=out_specs, check_vma=False)
```

time: 1310 us -> 173 us (0.13); the launches traced: 1300 us -> 172 us
  waiting for transfers between devices: 933 us -> 0 us
  Pallas kernels: 0 us -> 162 us
  starting transfers between devices: 116 us -> 0 us
  blocking collectives: 107 us -> 0 us
  local copies, waits for them, and re-layouts: 78.8 us -> 10.2 us
  other arithmetic: 41.1 us -> 0.06 us
  between operations: 14.3 us -> 0.08 us
    all_gather x4 -> x0, waiting for transfers between devices: 550 us -> none  [local(): lax.all_gather(flat_blocks.astype(jnp.bfloat16), 'col', axis=0, tiled=True)]
    all_to_all x8 -> x0, waiting for transfers between devices: 382 us -> none  [the longest x4 377 us: local(): lax.all_to_all(outgoing, 'col', split_axis=0, concat_axis=0, tiled=True)]
    pallas_call x0 -> x1, Pallas kernels: none -> 162 us  [local(): pl.pallas_call(functools.partial(kernel, owners, rows), out_shape=jax.Sha...]
    all_to_all x8 -> x0, starting transfers between devices: 116 us -> none  [the longest x4 68 us: local(): lax.all_to_all(outgoing, 'col', split_axis=0, concat_axis=0, tiled=True)]
    psum x8 -> x0, blocking collectives: 107 us -> none  [solve_blocks(): summed = lax.psum(partial_value, 'row')]
    scatter-add x8 -> x0, other arithmetic: 25.1 us -> none  [the longest x4 18.2 us: local(): jax.ops.segment_sum(incoming, landing, num_segments=slots_all + 1)]
    gather x4 -> x0, local copies, waits for them, and re-layouts: 24.3 us -> none  [local(): picked = jnp.take(whole_levels, targets[height], axis=0)]
    all_to_all x8 -> x0, local copies, waits for them, and re-layouts: 17.2 us -> none  [the longest x4 14.3 us: local(): lax.all_to_all(outgoing, 'col', split_axis=0, concat_axis=0, tiled=True)]
  transfers between devices with their start and end apart: 12 -> 0, of which waited for: 9 -> 0; matrix products, arithmetic and copies ran while one was open for 5% -> 0% of each run, Pallas kernels for 0% -> 0%
where the time goes in v1:
time: 173 us; the launch traced here: 172 us
  Pallas kernels  162 us (94%)
  local copies, waits for them, and re-layouts  10.2 us (6%)
    pallas_call x1, Pallas kernels, local(): pl.pallas_call(functools.partial(kernel, owners, rows), out_shape=jax.Sha...  162 us
    reshape x1, local copies, waits for them, and re-layouts, local(): bt = right_side.reshape(LEVELS, BPL, BS, cells, RW).transpose(3, 0, 4, 1, 2)  3.66 us

profile of v1, /device:TPU:1, one launch (start us, length us, event | category | flops | bytes accessed | tf_op | source)
XLA Modules:
  0.0 172.4 jit_solution(1206494333223975532)
XLA Ops:
  0.0 0.0 copy-start.1
  0.0 3.7 %reshape.30 = f32[5,2,64,8,8]{4,3,2,1,0:T(8,128)} reshape(f32[5,2,4096]{2,1,0:T(2,128)} %param.4) | data formatting | bytes 327680 | tf_op jit(solution)/shard_map/reshape | solution.py:402
  3.7 0.0 copy-start.2
  3.7 0.0 copy-start
  3.7 2.5 %copy.9.bt = f32[8,5,8,128]{3,2,1,0:T(8,128)S(1)} copy(f32[8,5,8,128]{2,0,3,1:T(8,128)} %bitcast.13) | data formatting | bytes 327680 | tf_op jit(solution)/shard_map/reshape | solution.py:403
  6.2 0.0 copy-done.1
  6.2 0.3 broadcast_in_dim.34
  6.4 0.2 broadcast_in_dim.35
  6.7 0.4 broadcast_in_dim.36
  7.0 0.1 broadcast_in_dim.31
  7.2 0.1 broadcast_in_dim.32
  7.3 0.0 copy-done.2
  7.3 0.1 tile.10
  7.4 0.1 tile.12
  7.5 0.0 copy-done
  7.5 162.0 %shard_map.46 = f32[8,5,8,128]{3,2,1,0:T(8,128)S(1)} custom-call(f32[8,5,8,128]{3,2,1,0:T(8,128)S(1)} %copy.9.bt, f32[5,128,128]{2,1,0:T(8,128)S(1)} %broadcast_select_fusion.dd, s32[8,128]{1,0:T(8,128)S(1)} %fusion.tr, bf16[4,128,512]{2,1,0:T(8,128)(2,1)S(1)} %bitcast.11), custom_call_target="tpu_custom_call" | custom-call | tf_op jit(solution)/shard_map/pallas_call | solution.py:415
  169.6 0.8 copy.10
  170.4 2.0 %reshape.34 = f32[5,2,4096]{2,1,0:T(2,128)} reshape(f32[5,2,64,8,8]{4,3,2,1,0:T(8,128)S(1)} %bitcast.12) | data formatting | bytes 327680 | tf_op jit(solution)/shard_map/reshape | solution.py:459
  (6 shorter events, 0.1 us)
Async XLA Ops:
  0.0 6.2 %copy-start.1 = (f32[5,2,4096]{2,1,0:T(2,128)S(1)}, f32[5,2,4096]{2,1,0:T(2,128)}, u32[]{:S(2)}) copy-start(f32[5,2,4096]{2,1,0:T(2,128)} %param.5) | copy-start | bytes 491524
  3.7 3.6 %copy-start.2 = (s32[4,2,8]{2,1,0:T(2,128)S(1)}, s32[4,2,8]{2,1,0:T(2,128)}, u32[]{:S(2)}) copy-start(s32[4,2,8]{2,1,0:T(2,128)} %param.7) | copy-start | bytes 772
  3.7 3.8 %copy-start = (bf16[4,2,64,512]{3,2,1,0:T(8,128)(2,1)S(1)}, bf16[4,2,64,512]{3,2,1,0:T(8,128)(2,1)}, u32[]{:S(2)}) copy-start(bf16[4,2,64,512]{3,2,1,0:T(8,128)(2,1)} %param.6) | copy-start | bytes 1572868

commit v2 on v1

v2 whole, which is shorter than its diff:
```python
import functools

import jax
import jax.numpy as jnp
from jax import lax
from jax.experimental import pallas as pl
from jax.experimental.pallas import tpu as pltpu
from jax.sharding import PartitionSpec as P

BS = 64
LEVELS = 5
BPL = 2
NNZ_DEV = 8
TLEV = 4
RW = 8
MESH = pl.DeviceIdType.MESH
F32 = jnp.float32
BF16 = jnp.bfloat16
NT_DIMS = (((1,), (1,)), ((), ()))
NN_DIMS = (((1,), (0,)), ((), ()))


def sizes(owners):
    nz = 16 if owners % 32 == 0 else owners // 4
    return owners // 2 // nz, nz


def split(value):
    high = value.astype(BF16)
    return high, (value - high.astype(F32)).astype(BF16)


def product(value, pair, dims):
    rows = value.shape[0]
    high, rest = split(value)
    both = jnp.concatenate([high.astype(F32), rest.astype(F32)], axis=0).astype(BF16)
    first = lax.dot_general(both, pair[0], dims, preferred_element_type=F32)
    second = lax.dot_general(high, pair[1], dims, preferred_element_type=F32)
    return first[:rows] + (first[rows:] + second)


def kernel(
    owners,
    rows,
    rs,
    di,
    tr,
    pan,
    out,
    trg,
    flip,
    bt,
    bu,
    ddc,
    pg,
    p0s,
    p0r,
    tbl,
    keepv,
    tbs,
    keeps,
    pd,
    cs,
    acc,
    sb,
    own,
    ry,
    sz,
    rz,
    ys,
    xu,
    xs,
    fx,
    osc,
    cell_sem,
    pan_sem,
    loc_sem,
    tab_sem,
    y_send,
    y_recv,
    z_send,
    z_recv,
    f_send,
    f_recv,
):
    ny, nz = sizes(owners)
    units = owners // 2
    cols = owners * BPL
    cells = 2 * rows
    per = BPL * NNZ_DEV
    tiles = cells * per
    chunks = (TLEV * cols + 127) // 128
    nfar = max(1, nz // 2 - 1)
    groups = ((0, nfar), (nfar, nz))
    col = lax.axis_index("col")
    x = lax.axis_index("row")
    c = col & 1
    z = (col // 2) & (nz - 1)
    y = col // (2 * nz)
    me = x * 2 + c

    def at(x_to, y_to, z_to, c_to):
        return {"row": x_to, "col": (y_to * nz + z_to) * 2 + c_to}

    def cell_peer(j):
        other = (me + j) & (cells - 1)
        return other, at(other // 2, y, z, other & 1)

    def y_peer(j):
        return at(x, (y + j) & (ny - 1), z, c)

    def step(p):
        half = (p + 1) // 2
        return nz // 2 + (half if p % 2 == 0 else -half)

    def facing(p):
        return p if step(p) in (0, nz // 2) else p + 1 if p % 2 == 1 else p - 1

    def z_peer(p):
        return at(x, y, (z + step(p)) & (nz - 1), c)

    def unit_of(j, p):
        return ((y + j) & (ny - 1)) * nz + ((z + step(p)) & (nz - 1))

    def send(src, dst, send_sem, recv_sem, device):
        pltpu.make_async_remote_copy(
            src_ref=src,
            dst_ref=dst,
            send_sem=send_sem,
            recv_sem=recv_sem,
            device_id=device,
            device_id_type=MESH,
        ).start()

    def settle(ref, sem):
        pltpu.make_async_copy(ref, ref, sem).wait()

    def low_of(count):
        return lax.broadcasted_iota(jnp.int32, (count, 128), 1) < BS

    low = low_of(RW)
    low32 = low_of(32)

    for t in range(TLEV):
        pltpu.make_async_copy(pan.at[t], pg.at[t, me], loc_sem.at[t]).start()

    barrier = pltpu.get_barrier_semaphore()

    def greet(device):
        pl.semaphore_signal(barrier, inc=1, device_id=device, device_id_type=MESH)

    for p in range(nz - 1):
        greet(z_peer(p))
    for j in range(1, ny):
        greet(y_peer(j))
    for j in range(1, cells):
        greet(cell_peer(j)[1])

    for t in range(LEVELS):
        for k in range(BPL):
            value = rs[t, pl.ds(k, 32, 2), :]
            flip[t, pl.ds(k * BS, 32, 2), :] = value
            flip[t, pl.ds(k * BS + 1, 32, 2), :] = pltpu.roll(value, BS, 1)
            value = di[t, pl.ds(k, 32, 2), :]
            turned = pltpu.roll(value, BS, 1)
            keep = low32 if k == 0 else jnp.logical_not(low32)
            for par in range(2):
                half = value if par == k else turned
                flip[LEVELS + t, pl.ds(k * BS + par, 32, 2), :] = jnp.where(keep, half, 0.0)
    cells_r = cells * RW
    for t in range(LEVELS):
        turned = flip[t].T
        for q in range(cells):
            bt[t, q] = turned[q * RW : (q + 1) * RW]
        high, rest = split(flip[LEVELS + t])
        ddc[c, t, 0] = high
        ddc[c, t, 1] = rest
    trg[me] = tr[...]
    for t in range(LEVELS):
        bu[c, t] = bt[t, me]

    right = bt[0].reshape(cells_r, 128)
    solved = product(right, (ddc[c, 0, 0], ddc[c, 0, 1]), NT_DIMS)
    pieces = []
    for q in range(cells):
        value = solved[q * RW : (q + 1) * RW]
        pieces += [jnp.where(low, value, 0.0), jnp.where(low, 0.0, value)]
    pltpu.make_async_copy(pan.at[0], pg.at[0, me], loc_sem.at[0]).wait()
    value = lax.dot_general(
        jnp.concatenate(pieces, axis=0).astype(BF16),
        pg[0, me],
        NN_DIMS,
        preferred_element_type=F32,
    ).astype(BF16)
    for q in range(cells):
        p0s[q] = value[q * 2 * RW : (q + 1) * 2 * RW]

    pl.semaphore_wait(barrier, cells - 1 + ny - 1 + nz - 1)

    for j in range(1, cells):
        other, device = cell_peer(j)
        send(tr, trg.at[me], cell_sem.at[0], cell_sem.at[1], device)
    for j in range(1, cells):
        other, device = cell_peer(j)
        send(p0s.at[other], p0r.at[me], cell_sem.at[6], cell_sem.at[7], device)
    core_peer = at(x, y, z, 1 - c)
    send(bt.at[:, me + 1 - 2 * c], bu.at[c], cell_sem.at[2], cell_sem.at[3], core_peer)
    send(ddc.at[c], ddc.at[c], cell_sem.at[4], cell_sem.at[5], core_peer)

    def send_panels(t):
        for j in range(1, cells):
            device = cell_peer(j)[1]
            send(pan.at[t], pg.at[t, me], pan_sem.at[0, t], pan_sem.at[1, t], device)

    send_panels(1)
    p0r[me] = p0s[me]

    settle(trg.at[pl.ds(0, cells - 1)], cell_sem.at[1])
    targets = trg[0]
    for j in range(1, cells):
        targets = targets + trg[j]
    square = (128, 128)
    above = lax.broadcasted_iota(jnp.int32, square, 0)
    lane = lax.broadcasted_iota(jnp.int32, square, 1)
    for t in range(TLEV):
        mine = jnp.broadcast_to(targets[t : t + 1, :], square)
        other = mine.T
        before = (other < mine) | ((other == mine) & (above < lane))
        rank = jnp.sum(before.astype(jnp.int32), axis=0, keepdims=True)
        placed = jnp.broadcast_to(rank, square).T == lane
        order = jnp.sum(jnp.where(placed, above, 0), axis=0, keepdims=True)
        ordered = jnp.sum(jnp.where(placed, other, 0), axis=0, keepdims=True)
        ordered8 = jnp.broadcast_to(ordered, (8, 128))
        first = lax.broadcasted_iota(jnp.int32, (8, 128), 1) == 0
        same = (ordered8 == pltpu.roll(ordered8, 1, 1)) & jnp.logical_not(first)
        keepv[t : t + 1, :] = same.astype(F32)[0:1]
        tbl[t : t + 1, :] = order
        source = jnp.clip(mine[0:1] - cols, 0, TLEV * cols - 1)
        tbl[TLEV + t : TLEV + t + 1, :] = source
        for chunk in range(t * cols // 128, chunks):
            slot = lane + (cols + chunk * 128)
            upto = jnp.sum((other <= slot).astype(jnp.int32), axis=0, keepdims=True)
            equal = jnp.sum((other == slot).astype(jnp.int32), axis=0, keepdims=True)
            row = 2 * TLEV + t * chunks + chunk
            tbl[row : row + 1, :] = jnp.where(equal > 0, upto - 1, 128)
    pltpu.make_async_copy(tbl, tbs, tab_sem.at[0]).start()
    pltpu.make_async_copy(keepv, keeps, tab_sem.at[1]).start()
    pltpu.make_async_copy(tbl, tbs, tab_sem.at[0]).wait()
    pltpu.make_async_copy(keepv, keeps, tab_sem.at[1]).wait()
    cs[128] = jnp.zeros((RW, 128), F32)

    def halves_of(t, level, u):
        number = (level - 1) * cols + u * 4
        row = 2 * TLEV + t * chunks + lax.shift_right_logical(number, 7)
        place = number & 127
        parts = [cs[tbs[row, place + k]] for k in range(4)]
        halves = [jnp.where(low, parts[0], parts[1]), jnp.where(low, parts[2], parts[3])]
        if t > 0:
            halves = [halves[h] + acc[level - 2, u * 2 + h] for h in range(2)]
        return halves

    def tile_pair(tile, value):
        turned = pltpu.roll(value, BS, 1)
        pd[tile] = jnp.where(low, value, turned)
        pd[tile + 1] = jnp.where(low, turned, value)

    def solve(t, core, remain, dims):
        return product(remain, (ddc[core, t, 0], ddc[core, t, 1]), dims)

    def forward(t, update):
        solved = []
        for core in range(2):
            remain = bu[core, t]
            if update is not None:
                remain = remain - update[core]
            value = solve(t, core, remain, NT_DIMS)
            ys[t, core] = value
            solved.append(value)
        return solved

    update = None
    for t in range(TLEV):
        if t == 0:
            settle(p0r.at[pl.ds(0, cells - 1)], cell_sem.at[7])
            for q in range(cells):
                value = p0r[q].astype(F32)
                for k in range(2):
                    for p in range(4):
                        part = value[k * RW : (k + 1) * RW, p * 128 : (p + 1) * 128]
                        tile_pair(q * per + k * NNZ_DEV + p * 2, part)
        else:
            solved = forward(t, update)
            nothing = jnp.zeros((RW, 128), F32)
            pieces = []
            for core in range(2):
                for k in range(2):
                    kept = jnp.where(low, solved[core], 0.0)
                    if k == 1:
                        kept = jnp.where(low, 0.0, solved[core])
                    side = [kept, nothing] if core == 0 else [nothing, kept]
                    pieces.append(jnp.concatenate(side, axis=1))
            vectors = jnp.concatenate(pieces, axis=0).astype(BF16)
            settle(pg.at[t, 0], loc_sem.at[t])
            settle(pg.at[t, pl.ds(0, cells - 1)], pan_sem.at[1, t])
            for group in range(rows):
                panel = pg[t, pl.ds(2 * group, 2)].reshape(4 * BS, NNZ_DEV * BS)
                value = lax.dot_general(vectors, panel, NN_DIMS, preferred_element_type=F32)
                for b in range(4):
                    for p in range(4):
                        part = value[b * RW : (b + 1) * RW, p * 128 : (p + 1) * 128]
                        tile_pair(group * 32 + b * 8 + p * 2, part)

        def scan(i, total, t=t):
            for k in range(16):
                place = i * 16 + k
                total = total * keeps[t, place] + pd[tbs[t, place]]
                cs[place] = total
            return total

        lax.fori_loop(0, tiles // 16, scan, jnp.zeros((RW, 128), F32))

        for g, (begin, end) in enumerate(groups):

            @pl.loop(0, ny - 1)
            def _(i, t=t, g=g, begin=begin, end=end):
                j = jnp.where(i == 0, ny // 2, jnp.where(i < ny // 2 + (ny == 2), i, i + 1))
                for p in range(begin, end):
                    halves = halves_of(t, t + 1, unit_of(j, p))
                    sb[t, j, p] = jnp.concatenate(halves, axis=0).astype(BF16)
                there = pl.ds(begin, end - begin)
                send(
                    sb.at[t, j, there],
                    ry.at[t, j - 1, there],
                    y_send.at[2 * t + g],
                    y_recv.at[2 * t + g],
                    y_peer(j),
                )

        for p in range(nz):
            halves = halves_of(t, t + 1, unit_of(0, p))
            own[p, 0] = halves[0]
            own[p, 1] = halves[1]
        if t + 2 < TLEV:
            send_panels(t + 2)
        for level in range(t + 2, LEVELS):

            @pl.loop(0, units // 4)
            def _(i, t=t, level=level):
                for k in range(4):
                    u = i * 4 + k
                    halves = halves_of(t, level, u)
                    acc[level - 2, u * 2] = halves[0]
                    acc[level - 2, u * 2 + 1] = halves[1]

        if t == 0:
            settle(bu.at[0], cell_sem.at[3])
            settle(ddc.at[0], cell_sem.at[5])
            forward(0, None)

        def partial(p, t=t):
            halves = []
            for h in range(2):
                value = own[p, h]
                for j in range(ny - 1):
                    value = value + ry[t, j, p].astype(F32)[h * RW : (h + 1) * RW]
                halves.append(value)
            return halves

        for g, (begin, end) in enumerate(groups):
            settle(ry.at[t, :, pl.ds(begin, end - begin)], y_recv.at[2 * t + g])
            for p in range(begin, min(end, nz - 1)):
                sz[t, p] = jnp.concatenate(partial(p), axis=0).astype(BF16)
                send(sz.at[t, p], rz.at[t, p], z_send.at[2 * t], z_recv.at[2 * t], z_peer(p))
        update = partial(nz - 1)
        settle(rz.at[t], z_recv.at[2 * t])
        for p in range(nz - 1):
            arrived = rz[t, p].astype(F32)
            update = [update[0] + arrived[:RW], update[1] + arrived[RW:]]

    send_panels(0)
    forward(TLEV, update)

    def finish(t):
        settle(osc.at[t, pl.ds(0, cells - 1)], f_recv.at[t])
        value = osc[t].reshape(cells_r, 128)
        if cells_r < 128:
            value = jnp.concatenate([value] * (128 // cells_r), axis=0)
        flip[t] = value.T
        for k in range(BPL):
            even = flip[t, pl.ds(k * BS, 32, 2), :]
            odd = flip[t, pl.ds(k * BS + 1, 32, 2), :]
            out[t, pl.ds(k, 32, 2), :] = jnp.where(low32, even, odd)

    for t in range(LEVELS - 1, -1, -1):
        if t < TLEV:
            if t == 0:
                settle(pg.at[0, pl.ds(0, cells - 1)], pan_sem.at[1, 0])
            weighted = None
            for group in range(rows):
                lines = []
                for b in range(4):
                    line = []
                    for p in range(4):
                        tile = group * 32 + b * 8 + p * 2
                        first = xs[tbs[TLEV + t, tile]]
                        second = xs[tbs[TLEV + t, tile + 1]]
                        line.append(jnp.where(low, first, second))
                    lines.append(jnp.concatenate(line, axis=1))
                picked = jnp.concatenate(lines, axis=0).astype(BF16)
                panel = pg[t, pl.ds(2 * group, 2)].reshape(4 * BS, NNZ_DEV * BS)
                value = lax.dot_general(picked, panel, NT_DIMS, preferred_element_type=F32)
                weighted = value if weighted is None else weighted + value
        results = []
        for core in range(2):
            remain = ys[t, core]
            if t < TLEV:
                lanes = slice(core * 128, core * 128 + 128)
                remain = remain - jnp.where(
                    low,
                    weighted[core * 16 : core * 16 + 8, lanes],
                    weighted[core * 16 + 8 : core * 16 + 16, lanes],
                )
            value = solve(t, core, remain, NN_DIMS)
            fx[t, core] = value
            results.append(value)
        n = TLEV + t - 1
        if t > 0:
            xu[t - 1, 0, nz - 1] = jnp.concatenate(results, axis=0).astype(BF16)
            for p in range(nz - 1):
                seen = facing(p)
                g = 0 if seen < nfar else 1
                send(
                    xu.at[t - 1, 0, nz - 1],
                    xu.at[t - 1, 0, seen],
                    z_send.at[2 * n],
                    z_recv.at[2 * n + g],
                    z_peer(p),
                )

        osc[t, me] = fx[t, c]
        for j in range(1, cells):
            other, device = cell_peer(j)
            send(fx.at[t, other & 1], osc.at[t, me], f_send, f_recv.at[t], device)
        if t + 1 < LEVELS:
            finish(t + 1)

        if t > 0:

            def expand(j, p, t=t):
                value = xu[t - 1, j, p].astype(F32)
                slot = (t - 1) * cols + unit_of(j, p) * 4
                for h in range(2):
                    half = value[h * RW : (h + 1) * RW]
                    turned = pltpu.roll(half, BS, 1)
                    xs[slot + 2 * h] = jnp.where(low, half, turned)
                    xs[slot + 2 * h + 1] = jnp.where(low, turned, half)

            for g, (begin, end) in reversed(list(enumerate(groups))):
                count = min(end, nz - 1) - begin
                if count > 0:
                    settle(xu.at[t - 1, 0, pl.ds(begin, count)], z_recv.at[2 * n + g])
                there = pl.ds(begin, end - begin)
                for j in range(1, ny):
                    send(
                        xu.at[t - 1, 0, there],
                        xu.at[t - 1, ny - j, there],
                        y_send.at[2 * n + g],
                        y_recv.at[2 * n + g],
                        y_peer(j),
                    )
                for p in range(begin, end):
                    expand(0, p)
            for g, (begin, end) in reversed(list(enumerate(groups))):
                there = pl.ds(begin, end - begin)
                settle(xu.at[t - 1, pl.ds(1, ny - 1), there], y_recv.at[2 * n + g])

                @pl.loop(1, ny)
                def _(j, begin=begin, end=end):
                    for p in range(begin, end):
                        expand(j, p)

    finish(0)

    settle(trg.at[pl.ds(0, cells - 1)], cell_sem.at[0])
    settle(bu.at[0], cell_sem.at[2])
    settle(ddc.at[0], cell_sem.at[4])
    settle(p0r.at[pl.ds(0, cells - 1)], cell_sem.at[6])
    for t in range(TLEV):
        settle(pg.at[t, pl.ds(0, cells - 1)], pan_sem.at[0, t])
        settle(rz.at[t], z_send.at[2 * t])
        settle(xu.at[t, 0, pl.ds(0, nz - 1)], z_send.at[2 * (TLEV + t)])
        for g, (begin, end) in enumerate(groups):
            there = pl.ds(begin, end - begin)
            settle(ry.at[t, :, there], y_send.at[2 * t + g])
            settle(xu.at[t, pl.ds(1, ny - 1), there], y_send.at[2 * (TLEV + t) + g])
    for t in range(LEVELS):
        settle(osc.at[t, pl.ds(0, cells - 1)], f_send)


def pairs_of(value):
    value = value.reshape(LEVELS, BPL, -1, 128).transpose(0, 2, 1, 3)
    return value.reshape(LEVELS, -1, 128)


def local(right_side, diag_inverse, panels, tile_rows):
    owners = lax.axis_size("col")
    rows = lax.axis_size("row")
    ny, nz = sizes(owners)
    units = owners // 2
    cols = owners * BPL
    cells = 2 * rows
    chunks = (TLEV * cols + 127) // 128
    table_rows = 2 * TLEV + TLEV * chunks
    me = lax.axis_index("row") * 2 + lax.axis_index("col") % 2
    pan = panels.reshape(TLEV, BPL * BS, NNZ_DEV * BS)
    per = BPL * NNZ_DEV
    spread = jnp.tile(tile_rows.reshape(TLEV, per), (2, 128 // per))
    lane = lax.broadcasted_iota(jnp.int32, (8, 128), 1)
    tr = jnp.where(lane // per == me, spread, 0)
    if cells * per < 128:
        tr = jnp.where(lane >= cells * per, 1 << 20, tr)
    vmem = pl.BlockSpec(memory_space=pltpu.VMEM)
    result = pl.pallas_call(
        functools.partial(kernel, owners, rows),
        out_shape=jax.ShapeDtypeStruct((LEVELS, BS, 128), F32),
        in_specs=[vmem, vmem, vmem, pl.BlockSpec(memory_space=pl.ANY)],
        out_specs=vmem,
        scratch_shapes=[
            pltpu.VMEM((cells, 8, 128), jnp.int32),
            pltpu.VMEM((2 * LEVELS, 128, 128), F32),
            pltpu.VMEM((LEVELS, cells, RW, 128), F32),
            pltpu.VMEM((2, LEVELS, RW, 128), F32),
            pltpu.VMEM((2, LEVELS, 2, 128, 128), BF16),
            pltpu.VMEM((TLEV, cells, BPL * BS, NNZ_DEV * BS), BF16),
            pltpu.VMEM((cells, 2 * RW, NNZ_DEV * BS), BF16),
            pltpu.VMEM((cells, 2 * RW, NNZ_DEV * BS), BF16),
            pltpu.VMEM((table_rows, 128), jnp.int32),
            pltpu.VMEM((8, 128), F32),
            pltpu.SMEM((table_rows, 128), jnp.int32),
            pltpu.SMEM((8, 128), F32),
            pltpu.VMEM((128, RW, 128), F32),
            pltpu.VMEM((129, RW, 128), F32),
            pltpu.VMEM((TLEV - 1, units * 2, RW, 128), F32),
            pltpu.VMEM((TLEV, ny, nz, 2 * RW, 128), BF16),
            pltpu.VMEM((nz, 2, RW, 128), F32),
            pltpu.VMEM((TLEV, ny - 1, nz, 2 * RW, 128), BF16),
            pltpu.VMEM((TLEV, nz - 1, 2 * RW, 128), BF16),
            pltpu.VMEM((TLEV, nz - 1, 2 * RW, 128), BF16),
            pltpu.VMEM((LEVELS, 2, RW, 128), F32),
            pltpu.VMEM((TLEV, ny, nz, 2 * RW, 128), BF16),
            pltpu.VMEM((TLEV * cols, RW, 128), F32),
            pltpu.VMEM((LEVELS, 2, RW, 128), F32),
            pltpu.VMEM((LEVELS, cells, RW, 128), F32),
            pltpu.SemaphoreType.DMA((8,)),
            pltpu.SemaphoreType.DMA((2, TLEV)),
            pltpu.SemaphoreType.DMA((TLEV,)),
            pltpu.SemaphoreType.DMA((2,)),
            pltpu.SemaphoreType.DMA((4 * TLEV,)),
            pltpu.SemaphoreType.DMA((4 * TLEV,)),
            pltpu.SemaphoreType.DMA((4 * TLEV,)),
            pltpu.SemaphoreType.DMA((4 * TLEV,)),
            pltpu.SemaphoreType.DMA,
            pltpu.SemaphoreType.DMA((LEVELS,)),
        ],
        compiler_params=pltpu.CompilerParams(
            collective_id=0, has_side_effects=True, vmem_limit_bytes=40 * 1024 * 1024
        ),
    )(pairs_of(right_side), pairs_of(diag_inverse), tr, pan)
    result = result.reshape(LEVELS, -1, BPL, 128).transpose(0, 2, 1, 3)
    return result.reshape(LEVELS, BPL, -1)


def solution(mesh):
    in_specs = (
        P(None, "col", None),
        P(None, "col", None),
        P(None, "col", None, "row"),
        P(None, "col", "row"),
    )
    out_specs = P(None, "col", None)
    return jax.shard_map(local, mesh=mesh, in_specs=in_specs, out_specs=out_specs, check_vma=False)
```

time: 173 us -> 128 us (0.74)
  Pallas kernels: 162 us -> 124 us
  local copies, waits for them, and re-layouts: 10.2 us -> 4.37 us
    pallas_call x1, Pallas kernels: 162 us -> 124 us  [local(): pl.pallas_call(functools.partial(kernel, owners, rows), out_shape=jax.Sha...]
    reshape x4 -> x0, local copies, waits for them, and re-layouts: 9.01 us -> none  [the longest x1 3.66 us: local(): bt = right_side.reshape(LEVELS, BPL, BS, cells, RW).transpose(3, 0, 4, 1, 2)]
    unnamed x6 -> x9, local copies, waits for them, and re-layouts: 0.01 us -> 4.2 us
where the time goes in v2:
time: 128 us
  Pallas kernels  124 us (97%)
  local copies, waits for them, and re-layouts  4.37 us (3%)
    pallas_call x1, Pallas kernels, local(): pl.pallas_call(functools.partial(kernel, owners, rows), out_shape=jax.Sha...  124 us
    unnamed x9, local copies, waits for them, and re-layouts  4.2 us

profile of v2, /device:TPU:1, one launch (start us, length us, event | category | flops | bytes accessed | tf_op | source)
XLA Modules:
  0.0 128.2 jit_solution(5208404267779872458)
XLA Ops:
  0.0 0.0 copy-start.3
  0.0 0.7 copy-done.3
  0.7 0.1 tile.10
  0.8 0.1 tile.12
  0.9 0.0 copy-start
  0.9 1.0 copy-done
  1.9 0.0 copy-start.1
  1.9 0.9 copy-done.1
  2.8 0.0 copy-start.2
  2.8 0.9 copy-done.2
  3.7 123.8 %shard_map.46 = f32[5,64,128]{2,1,0:T(8,128)S(1)} custom-call(f32[5,64,128]{2,1,0:T(8,128)S(1)} %bitcast.20, f32[5,64,128]{2,1,0:T(8,128)S(1)} %bitcast.21, s32[8,128]{1,0:T(8,128)S(1)} %fusion.tr, bf16[4,128,512]{2,1,0:T(8,128)(2,1)S(1)} %bitcast.19), custom_call_target="tpu_custom_call" | custom-call | tf_op jit(solution)/shard_map/pallas_call | solution.py:523
  127.6 0.7 copy.9
  (4 shorter events, 0.0 us)
Async XLA Ops:
  0.0 0.7 copy-start.3
  0.9 1.0 copy-start
  1.9 0.9 copy-start.1
  2.8 0.9 copy-start.2

commit v3 on v2

--- a/solution.py
+++ b/solution.py
@@ -16,6 +16,7 @@
 MESH = pl.DeviceIdType.MESH
 F32 = jnp.float32
 BF16 = jnp.bfloat16
+BOUNDS = (0, 3, 9, 16)
 NT_DIMS = (((1,), (1,)), ((), ()))
 NN_DIMS = (((1,), (0,)), ((), ()))
 
@@ -23,6 +24,11 @@
 def sizes(owners):
     nz = 16 if owners % 32 == 0 else owners // 4
     return owners // 2 // nz, nz
+
+
+def groups_of(nz):
+    bounds = BOUNDS if nz == 16 else (0, max(1, nz // 2 - 1), nz)
+    return tuple(zip(bounds[:-1], bounds[1:]))
 
 
 def split(value):
@@ -42,11 +48,13 @@
 def kernel(
     owners,
     rows,
-    rs,
-    di,
+    rs_far,
+    di_far,
     tr,
     pan,
     out,
+    rs,
+    di,
     trg,
     flip,
     bt,
@@ -90,8 +98,8 @@
     per = BPL * NNZ_DEV
     tiles = cells * per
     chunks = (TLEV * cols + 127) // 128
-    nfar = max(1, nz // 2 - 1)
-    groups = ((0, nfar), (nfar, nz))
+    groups = groups_of(nz)
+    parts = len(groups)
     col = lax.axis_index("col")
     x = lax.axis_index("row")
     c = col & 1
@@ -141,6 +149,9 @@
     low = low_of(RW)
     low32 = low_of(32)
 
+    pltpu.make_async_copy(rs_far, rs, loc_sem.at[TLEV]).start()
+    pltpu.make_async_copy(di_far, di, loc_sem.at[TLEV + 1]).start()
+    pltpu.make_async_copy(tr, trg.at[me], loc_sem.at[TLEV + 2]).start()
     for t in range(TLEV):
         pltpu.make_async_copy(pan.at[t], pg.at[t, me], loc_sem.at[t]).start()
 
@@ -156,6 +167,9 @@
     for j in range(1, cells):
         greet(cell_peer(j)[1])
 
+    pltpu.make_async_copy(rs_far, rs, loc_sem.at[TLEV]).wait()
+    pltpu.make_async_copy(di_far, di, loc_sem.at[TLEV + 1]).wait()
+    pltpu.make_async_copy(tr, trg.at[me], loc_sem.at[TLEV + 2]).wait()
     for t in range(LEVELS):
         for k in range(BPL):
             value = rs[t, pl.ds(k, 32, 2), :]
@@ -175,7 +189,6 @@
         high, rest = split(flip[LEVELS + t])
         ddc[c, t, 0] = high
         ddc[c, t, 1] = rest
-    trg[me] = tr[...]
     for t in range(LEVELS):
         bu[c, t] = bt[t, me]
 
@@ -216,9 +229,10 @@
     p0r[me] = p0s[me]
 
     settle(trg.at[pl.ds(0, cells - 1)], cell_sem.at[1])
-    targets = trg[0]
-    for j in range(1, cells):
-        targets = targets + trg[j]
+    pieces = [trg[q, :, k, :] for q in range(cells) for k in range(BPL)]
+    if tiles < 128:
+        pieces.append(jnp.full((TLEV, 128 - tiles), 1 << 20, jnp.int32))
+    targets = jnp.concatenate(pieces, axis=1)
     square = (128, 128)
     above = lax.broadcasted_iota(jnp.int32, square, 0)
     lane = lax.broadcasted_iota(jnp.int32, square, 1)
@@ -331,8 +345,8 @@
                 send(
                     sb.at[t, j, there],
                     ry.at[t, j - 1, there],
-                    y_send.at[2 * t + g],
-                    y_recv.at[2 * t + g],
+                    y_send.at[parts * t + g],
+                    y_recv.at[parts * t + g],
                     y_peer(j),
                 )
 
@@ -367,12 +381,12 @@
             return halves
 
         for g, (begin, end) in enumerate(groups):
-            settle(ry.at[t, :, pl.ds(begin, end - begin)], y_recv.at[2 * t + g])
+            settle(ry.at[t, :, pl.ds(begin, end - begin)], y_recv.at[parts * t + g])
             for p in range(begin, min(end, nz - 1)):
                 sz[t, p] = jnp.concatenate(partial(p), axis=0).astype(BF16)
-                send(sz.at[t, p], rz.at[t, p], z_send.at[2 * t], z_recv.at[2 * t], z_peer(p))
+                send(sz.at[t, p], rz.at[t, p], z_send.at[parts * t], z_recv.at[parts * t], z_peer(p))
         update = partial(nz - 1)
-        settle(rz.at[t], z_recv.at[2 * t])
+        settle(rz.at[t], z_recv.at[parts * t])
         for p in range(nz - 1):
             arrived = rz[t, p].astype(F32)
             update = [update[0] + arrived[:RW], update[1] + arrived[RW:]]
@@ -428,12 +442,12 @@
             xu[t - 1, 0, nz - 1] = jnp.concatenate(results, axis=0).astype(BF16)
             for p in range(nz - 1):
                 seen = facing(p)
-                g = 0 if seen < nfar else 1
+                g = [begin <= seen < end for begin, end in groups].index(True)
                 send(
                     xu.at[t - 1, 0, nz - 1],
                     xu.at[t - 1, 0, seen],
-                    z_send.at[2 * n],
-                    z_recv.at[2 * n + g],
+                    z_send.at[parts * n],
+                    z_recv.at[parts * n + g],
                     z_peer(p),
                 )
 
@@ -458,21 +472,21 @@
             for g, (begin, end) in reversed(list(enumerate(groups))):
                 count = min(end, nz - 1) - begin
                 if count > 0:
-                    settle(xu.at[t - 1, 0, pl.ds(begin, count)], z_recv.at[2 * n + g])
+                    settle(xu.at[t - 1, 0, pl.ds(begin, count)], z_recv.at[parts * n + g])
                 there = pl.ds(begin, end - begin)
                 for j in range(1, ny):
                     send(
                         xu.at[t - 1, 0, there],
                         xu.at[t - 1, ny - j, there],
-                        y_send.at[2 * n + g],
-                        y_recv.at[2 * n + g],
+                        y_send.at[parts * n + g],
+                        y_recv.at[parts * n + g],
                         y_peer(j),
                     )
                 for p in range(begin, end):
                     expand(0, p)
             for g, (begin, end) in reversed(list(enumerate(groups))):
                 there = pl.ds(begin, end - begin)
-                settle(xu.at[t - 1, pl.ds(1, ny - 1), there], y_recv.at[2 * n + g])
+                settle(xu.at[t - 1, pl.ds(1, ny - 1), there], y_recv.at[parts * n + g])
 
                 @pl.loop(1, ny)
                 def _(j, begin=begin, end=end):
@@ -487,12 +501,12 @@
     settle(p0r.at[pl.ds(0, cells - 1)], cell_sem.at[6])
     for t in range(TLEV):
         settle(pg.at[t, pl.ds(0, cells - 1)], pan_sem.at[0, t])
-        settle(rz.at[t], z_send.at[2 * t])
-        settle(xu.at[t, 0, pl.ds(0, nz - 1)], z_send.at[2 * (TLEV + t)])
+        settle(rz.at[t], z_send.at[parts * t])
+        settle(xu.at[t, 0, pl.ds(0, nz - 1)], z_send.at[parts * (TLEV + t)])
         for g, (begin, end) in enumerate(groups):
             there = pl.ds(begin, end - begin)
-            settle(ry.at[t, :, there], y_send.at[2 * t + g])
-            settle(xu.at[t, pl.ds(1, ny - 1), there], y_send.at[2 * (TLEV + t) + g])
+            settle(ry.at[t, :, there], y_send.at[parts * t + g])
+            settle(xu.at[t, pl.ds(1, ny - 1), there], y_send.at[parts * (TLEV + t) + g])
     for t in range(LEVELS):
         settle(osc.at[t, pl.ds(0, cells - 1)], f_send)
 
@@ -506,27 +520,24 @@
     owners = lax.axis_size("col")
     rows = lax.axis_size("row")
     ny, nz = sizes(owners)
+    parts = len(groups_of(nz))
     units = owners // 2
     cols = owners * BPL
     cells = 2 * rows
     chunks = (TLEV * cols + 127) // 128
     table_rows = 2 * TLEV + TLEV * chunks
-    me = lax.axis_index("row") * 2 + lax.axis_index("col") % 2
     pan = panels.reshape(TLEV, BPL * BS, NNZ_DEV * BS)
-    per = BPL * NNZ_DEV
-    spread = jnp.tile(tile_rows.reshape(TLEV, per), (2, 128 // per))
-    lane = lax.broadcasted_iota(jnp.int32, (8, 128), 1)
-    tr = jnp.where(lane // per == me, spread, 0)
-    if cells * per < 128:
-        tr = jnp.where(lane >= cells * per, 1 << 20, tr)
     vmem = pl.BlockSpec(memory_space=pltpu.VMEM)
+    far = pl.BlockSpec(memory_space=pltpu.HBM)
     result = pl.pallas_call(
         functools.partial(kernel, owners, rows),
         out_shape=jax.ShapeDtypeStruct((LEVELS, BS, 128), F32),
-        in_specs=[vmem, vmem, vmem, pl.BlockSpec(memory_space=pl.ANY)],
+        in_specs=[far, far, far, far],
         out_specs=vmem,
         scratch_shapes=[
-            pltpu.VMEM((cells, 8, 128), jnp.int32),
+            pltpu.VMEM((LEVELS, BS, 128), F32),
+            pltpu.VMEM((LEVELS, BS, 128), F32),
+            pltpu.VMEM((cells, TLEV, BPL, NNZ_DEV), jnp.int32),
             pltpu.VMEM((2 * LEVELS, 128, 128), F32),
             pltpu.VMEM((LEVELS, cells, RW, 128), F32),
             pltpu.VMEM((2, LEVELS, RW, 128), F32),
@@ -553,19 +564,19 @@
             pltpu.VMEM((LEVELS, cells, RW, 128), F32),
             pltpu.SemaphoreType.DMA((8,)),
             pltpu.SemaphoreType.DMA((2, TLEV)),
-            pltpu.SemaphoreType.DMA((TLEV,)),
+            pltpu.SemaphoreType.DMA((TLEV + 3,)),
             pltpu.SemaphoreType.DMA((2,)),
-            pltpu.SemaphoreType.DMA((4 * TLEV,)),
-            pltpu.SemaphoreType.DMA((4 * TLEV,)),
-            pltpu.SemaphoreType.DMA((4 * TLEV,)),
-            pltpu.SemaphoreType.DMA((4 * TLEV,)),
+            pltpu.SemaphoreType.DMA((2 * TLEV * parts,)),
+            pltpu.SemaphoreType.DMA((2 * TLEV * parts,)),
+            pltpu.SemaphoreType.DMA((2 * TLEV * parts,)),
+            pltpu.SemaphoreType.DMA((2 * TLEV * parts,)),
             pltpu.SemaphoreType.DMA,
             pltpu.SemaphoreType.DMA((LEVELS,)),
         ],
         compiler_params=pltpu.CompilerParams(
-            collective_id=0, has_side_effects=True, vmem_limit_bytes=40 * 1024 * 1024
+            collective_id=0, has_side_effects=True, vmem_limit_bytes=58 * 1024 * 1024
         ),
-    )(pairs_of(right_side), pairs_of(diag_inverse), tr, pan)
+    )(pairs_of(right_side), pairs_of(diag_inverse), tile_rows, pan)
     result = result.reshape(LEVELS, -1, BPL, 128).transpose(0, 2, 1, 3)
     return result.reshape(LEVELS, BPL, -1)
 

time: 128 us -> 123 us (0.961)
  Pallas kernels: 124 us -> 121 us
  local copies, waits for them, and re-layouts: 4.37 us -> 1.59 us
    unnamed x9 -> x1, local copies, waits for them, and re-layouts: 4.2 us -> 1.59 us
    pallas_call x1, Pallas kernels: 124 us -> 121 us  [local(): pl.pallas_call(functools.partial(kernel, owners, rows), out_shape=jax.Sha...]
where the time goes in v3:
time: 123 us
  Pallas kernels  121 us (98%)
  local copies, waits for them, and re-layouts  1.59 us (1%)
    pallas_call x1, Pallas kernels, local(): pl.pallas_call(functools.partial(kernel, owners, rows), out_shape=jax.Sha...  121 us

profile of v3, /device:TPU:1, one launch (start us, length us, event | category | flops | bytes accessed | tf_op | source)
XLA Modules:
  0.0 122.9 jit_solution(15890006475489155905)
XLA Ops:
  0.0 121.3 %shard_map.46 = f32[5,64,128]{2,1,0:T(8,128)} custom-call(f32[5,64,128]{2,1,0:T(8,128)} %bitcast.18, f32[5,64,128]{2,1,0:T(8,128)} %bitcast.19, s32[4,2,8]{2,1,0:T(2,128)} %tr.1, bf16[4,128,512]{2,1,0:T(8,128)(2,1)} %bitcast.17), custom_call_target="tpu_custom_call" | custom-call | tf_op jit(solution)/shard_map/pallas_call | solution.py:532
  121.3 1.6 %copy.9 = f32[5,2,4096]{2,1,0:T(2,128)} copy(f32[5,2,4096]{2,1,0:T(2,128)} %bitcast.16) | data formatting | bytes 327680

commit v4 on v3

--- a/solution.py
+++ b/solution.py
@@ -236,7 +236,7 @@
     square = (128, 128)
     above = lax.broadcasted_iota(jnp.int32, square, 0)
     lane = lax.broadcasted_iota(jnp.int32, square, 1)
-    for t in range(TLEV):
+    def table(t):
         mine = jnp.broadcast_to(targets[t : t + 1, :], square)
         other = mine.T
         before = (other < mine) | ((other == mine) & (above < lane))
@@ -247,28 +247,29 @@
         ordered8 = jnp.broadcast_to(ordered, (8, 128))
         first = lax.broadcasted_iota(jnp.int32, (8, 128), 1) == 0
         same = (ordered8 == pltpu.roll(ordered8, 1, 1)) & jnp.logical_not(first)
-        keepv[t : t + 1, :] = same.astype(F32)[0:1]
-        tbl[t : t + 1, :] = order
+        keepv[t, 0:1, :] = same.astype(F32)[0:1]
+        tbl[t, 0:1, :] = order
         source = jnp.clip(mine[0:1] - cols, 0, TLEV * cols - 1)
-        tbl[TLEV + t : TLEV + t + 1, :] = source
+        tbl[t, 1:2, :] = source
         for chunk in range(t * cols // 128, chunks):
             slot = lane + (cols + chunk * 128)
             upto = jnp.sum((other <= slot).astype(jnp.int32), axis=0, keepdims=True)
             equal = jnp.sum((other == slot).astype(jnp.int32), axis=0, keepdims=True)
-            row = 2 * TLEV + t * chunks + chunk
-            tbl[row : row + 1, :] = jnp.where(equal > 0, upto - 1, 128)
-    pltpu.make_async_copy(tbl, tbs, tab_sem.at[0]).start()
-    pltpu.make_async_copy(keepv, keeps, tab_sem.at[1]).start()
-    pltpu.make_async_copy(tbl, tbs, tab_sem.at[0]).wait()
-    pltpu.make_async_copy(keepv, keeps, tab_sem.at[1]).wait()
+            tbl[t, 2 + chunk : 3 + chunk, :] = jnp.where(equal > 0, upto - 1, 128)
+        pltpu.make_async_copy(tbl.at[t], tbs.at[t], tab_sem.at[0]).start()
+        pltpu.make_async_copy(keepv.at[t], keeps.at[t], tab_sem.at[1]).start()
+        pltpu.make_async_copy(tbl.at[t], tbs.at[t], tab_sem.at[0]).wait()
+        pltpu.make_async_copy(keepv.at[t], keeps.at[t], tab_sem.at[1]).wait()
+
+    table(0)
     cs[128] = jnp.zeros((RW, 128), F32)
 
     def halves_of(t, level, u):
         number = (level - 1) * cols + u * 4
-        row = 2 * TLEV + t * chunks + lax.shift_right_logical(number, 7)
+        row = 2 + lax.shift_right_logical(number, 7)
         place = number & 127
-        parts = [cs[tbs[row, place + k]] for k in range(4)]
-        halves = [jnp.where(low, parts[0], parts[1]), jnp.where(low, parts[2], parts[3])]
+        found = [cs[tbs[t, row, place + k]] for k in range(4)]
+        halves = [jnp.where(low, found[0], found[1]), jnp.where(low, found[2], found[3])]
         if t > 0:
             halves = [halves[h] + acc[level - 2, u * 2 + h] for h in range(2)]
         return halves
@@ -327,7 +328,7 @@
         def scan(i, total, t=t):
             for k in range(16):
                 place = i * 16 + k
-                total = total * keeps[t, place] + pd[tbs[t, place]]
+                total = total * keeps[t, 0, place] + pd[tbs[t, 0, place]]
                 cs[place] = total
             return total
 
@@ -354,23 +355,6 @@
             halves = halves_of(t, t + 1, unit_of(0, p))
             own[p, 0] = halves[0]
             own[p, 1] = halves[1]
-        if t + 2 < TLEV:
-            send_panels(t + 2)
-        for level in range(t + 2, LEVELS):
-
-            @pl.loop(0, units // 4)
-            def _(i, t=t, level=level):
-                for k in range(4):
-                    u = i * 4 + k
-                    halves = halves_of(t, level, u)
-                    acc[level - 2, u * 2] = halves[0]
-                    acc[level - 2, u * 2 + 1] = halves[1]
-
-        if t == 0:
-            settle(bu.at[0], cell_sem.at[3])
-            settle(ddc.at[0], cell_sem.at[5])
-            forward(0, None)
-
         def partial(p, t=t):
             halves = []
             for h in range(2):
@@ -384,12 +368,40 @@
             settle(ry.at[t, :, pl.ds(begin, end - begin)], y_recv.at[parts * t + g])
             for p in range(begin, min(end, nz - 1)):
                 sz[t, p] = jnp.concatenate(partial(p), axis=0).astype(BF16)
-                send(sz.at[t, p], rz.at[t, p], z_send.at[parts * t], z_recv.at[parts * t], z_peer(p))
+                send(
+                    sz.at[t, p],
+                    rz.at[t, p],
+                    z_send.at[parts * t],
+                    z_recv.at[parts * t + g],
+                    z_peer(p),
+                )
+        if t + 2 < TLEV:
+            send_panels(t + 2)
+        for level in range(t + 2, LEVELS):
+
+            @pl.loop(0, units // 4)
+            def _(i, t=t, level=level):
+                for k in range(4):
+                    u = i * 4 + k
+                    halves = halves_of(t, level, u)
+                    acc[level - 2, u * 2] = halves[0]
+                    acc[level - 2, u * 2 + 1] = halves[1]
+
+        if t == 0:
+            settle(bu.at[0], cell_sem.at[3])
+            settle(ddc.at[0], cell_sem.at[5])
+            forward(0, None)
+        if t + 1 < TLEV:
+            table(t + 1)
+
         update = partial(nz - 1)
-        settle(rz.at[t], z_recv.at[parts * t])
-        for p in range(nz - 1):
-            arrived = rz[t, p].astype(F32)
-            update = [update[0] + arrived[:RW], update[1] + arrived[RW:]]
+        for g, (begin, end) in reversed(list(enumerate(groups))):
+            count = min(end, nz - 1) - begin
+            if count > 0:
+                settle(rz.at[t, pl.ds(begin, count)], z_recv.at[parts * t + g])
+            for p in range(begin, begin + count):
+                arrived = rz[t, p].astype(F32)
+                update = [update[0] + arrived[:RW], update[1] + arrived[RW:]]
 
     send_panels(0)
     forward(TLEV, update)
@@ -416,8 +428,8 @@
                     line = []
                     for p in range(4):
                         tile = group * 32 + b * 8 + p * 2
-                        first = xs[tbs[TLEV + t, tile]]
-                        second = xs[tbs[TLEV + t, tile + 1]]
+                        first = xs[tbs[t, 1, tile]]
+                        second = xs[tbs[t, 1, tile + 1]]
                         line.append(jnp.where(low, first, second))
                     lines.append(jnp.concatenate(line, axis=1))
                 picked = jnp.concatenate(lines, axis=0).astype(BF16)
@@ -525,7 +537,7 @@
     cols = owners * BPL
     cells = 2 * rows
     chunks = (TLEV * cols + 127) // 128
-    table_rows = 2 * TLEV + TLEV * chunks
+    table_rows = (2 + chunks + 7) // 8 * 8
     pan = panels.reshape(TLEV, BPL * BS, NNZ_DEV * BS)
     vmem = pl.BlockSpec(memory_space=pltpu.VMEM)
     far = pl.BlockSpec(memory_space=pltpu.HBM)
@@ -545,10 +557,10 @@
             pltpu.VMEM((TLEV, cells, BPL * BS, NNZ_DEV * BS), BF16),
             pltpu.VMEM((cells, 2 * RW, NNZ_DEV * BS), BF16),
             pltpu.VMEM((cells, 2 * RW, NNZ_DEV * BS), BF16),
-            pltpu.VMEM((table_rows, 128), jnp.int32),
-            pltpu.VMEM((8, 128), F32),
-            pltpu.SMEM((table_rows, 128), jnp.int32),
-            pltpu.SMEM((8, 128), F32),
+            pltpu.VMEM((TLEV, table_rows, 128), jnp.int32),
+            pltpu.VMEM((TLEV, 8, 128), F32),
+            pltpu.SMEM((TLEV, table_rows, 128), jnp.int32),
+            pltpu.SMEM((TLEV, 8, 128), F32),
             pltpu.VMEM((128, RW, 128), F32),
             pltpu.VMEM((129, RW, 128), F32),
             pltpu.VMEM((TLEV - 1, units * 2, RW, 128), F32),

time: 123 us -> 123 us (level)
  no operation moved by 1% of the time
where the time goes in v4:
time: 123 us; the launch traced here: 122 us
  Pallas kernels  121 us (98%)
  local copies, waits for them, and re-layouts  1.59 us (1%)
    pallas_call x1, Pallas kernels, local(): pl.pallas_call(functools.partial(kernel, owners, rows), out_shape=jax.Sha...  121 us

profile of v4, /device:TPU:1, one launch (start us, length us, event | category | flops | bytes accessed | tf_op | source)
XLA Modules:
  0.0 122.5 jit_solution(13618589709284281858)
XLA Ops:
  0.0 120.9 %shard_map.46 = f32[5,64,128]{2,1,0:T(8,128)} custom-call(f32[5,64,128]{2,1,0:T(8,128)} %bitcast.18, f32[5,64,128]{2,1,0:T(8,128)} %bitcast.19, s32[4,2,8]{2,1,0:T(2,128)} %tr.1, bf16[4,128,512]{2,1,0:T(8,128)(2,1)} %bitcast.17), custom_call_target="tpu_custom_call" | custom-call | tf_op jit(solution)/shard_map/pallas_call | solution.py:544
  120.9 1.6 %copy.9 = f32[5,2,4096]{2,1,0:T(2,128)} copy(f32[5,2,4096]{2,1,0:T(2,128)} %bitcast.16) | data formatting | bytes 327680

commit v5 on v4

--- a/solution.py
+++ b/solution.py
@@ -258,6 +258,8 @@
             tbl[t, 2 + chunk : 3 + chunk, :] = jnp.where(equal > 0, upto - 1, 128)
         pltpu.make_async_copy(tbl.at[t], tbs.at[t], tab_sem.at[0]).start()
         pltpu.make_async_copy(keepv.at[t], keeps.at[t], tab_sem.at[1]).start()
+
+    def table_done(t):
         pltpu.make_async_copy(tbl.at[t], tbs.at[t], tab_sem.at[0]).wait()
         pltpu.make_async_copy(keepv.at[t], keeps.at[t], tab_sem.at[1]).wait()
 
@@ -325,14 +327,16 @@
                         part = value[b * RW : (b + 1) * RW, p * 128 : (p + 1) * 128]
                         tile_pair(group * 32 + b * 8 + p * 2, part)
 
+        table_done(t)
+
         def scan(i, total, t=t):
-            for k in range(16):
-                place = i * 16 + k
+            for k in range(32):
+                place = i * 32 + k
                 total = total * keeps[t, 0, place] + pd[tbs[t, 0, place]]
                 cs[place] = total
             return total
 
-        lax.fori_loop(0, tiles // 16, scan, jnp.zeros((RW, 128), F32))
+        lax.fori_loop(0, tiles // 32, scan, jnp.zeros((RW, 128), F32))
 
         for g, (begin, end) in enumerate(groups):
 

time: 123 us -> 123 us (level)
  no operation moved by 1% of the time
where the time goes in v5:
time: 123 us; the launch traced here: 122 us
  Pallas kernels  121 us (98%)
  local copies, waits for them, and re-layouts  1.59 us (1%)
    pallas_call x1, Pallas kernels, local(): pl.pallas_call(functools.partial(kernel, owners, rows), out_shape=jax.Sha...  121 us

profile of v5, /device:TPU:1, one launch (start us, length us, event | category | flops | bytes accessed | tf_op | source)
XLA Modules:
  0.0 122.5 jit_solution(3596587208812222469)
XLA Ops:
  0.0 120.9 %shard_map.46 = f32[5,64,128]{2,1,0:T(8,128)} custom-call(f32[5,64,128]{2,1,0:T(8,128)} %bitcast.18, f32[5,64,128]{2,1,0:T(8,128)} %bitcast.19, s32[4,2,8]{2,1,0:T(2,128)} %tr.1, bf16[4,128,512]{2,1,0:T(8,128)(2,1)} %bitcast.17), custom_call_target="tpu_custom_call" | custom-call | tf_op jit(solution)/shard_map/pallas_call | solution.py:548
  120.9 1.6 %copy.9 = f32[5,2,4096]{2,1,0:T(2,128)} copy(f32[5,2,4096]{2,1,0:T(2,128)} %bitcast.16) | data formatting | bytes 327680
